TPU v7x, 32 devices: a whole 2x2x4 slice. The times are simulated.
32 devices in a mesh: groups: 2 (over y), team: 4 (over z), rep: 4 (over x, core).
Axes of the slice: x: 2, y: 2, z: 4, core: 2. Of those that a mesh axis runs over, the one named last changes fastest.
Arguments:
- omega_rows: float32 [128, 32768], P(('groups', 'team'), 'rep'), parts along dimension 0, as said below
- covariance_columns: float32 [32768, 2048], P('rep', ('groups', 'team')), parts along dimension 1, may hold values from -0.03125 to 0.03125
- tile_offsets: int32 [8], P(('groups', 'team')), parts along dimension 0, may hold values from 0 to 32512, as said below
Outputs:
- new_omega: float32 [64, 2048], P('rep', ('groups', 'team')), parts along dimension 1
There are 2 independent parts, one for each index of `groups`. A program takes and returns all parts, laid end to end along the dimension named above; each array names one. Nothing has to cross between parts.
Inputs may be any that keep to these rules, and one draw needn't show every extreme that they name: `tile_offsets`: distinct multiples of 256; both 0 and 32512 occur. `omega_rows`: entries with column equal to row lie in 1 to 2.
All inputs are finite; a program needn't handle non-finite values.
Results may differ from a plain program's by a relative error of at most 0.0003.
Values sent between devices are 32-bit elements; how exact they have to be, the bound alone decides.
A program may use at most 64 MiB of HBM per device.

v0:
```python
import jax
import jax.numpy as jnp
from jax import lax
from jax.sharding import PartitionSpec as P

step_size = 0.5
penalty = 0.1


def shifted(array, axis, by):
    devices = lax.axis_size(axis)
    return lax.ppermute(array, axis, [(i, (i + by) % devices) for i in range(devices)])


def from_root(array, axis, root):
    mine = lax.axis_index(axis) == root
    return lax.psum(jnp.where(mine, array, jnp.zeros_like(array)), axis)


def per_device(omega_rows, covariance_columns, tile_offsets):
    team_count = lax.axis_size("team")
    rep_count = lax.axis_size("rep")
    team_index = lax.axis_index("team")
    rep_index = lax.axis_index("rep")
    block_rows, part_width = omega_rows.shape
    tile_width = covariance_columns.shape[1]
    all_rows = block_rows * team_count
    rows_share = all_rows // rep_count
    offset = tile_offsets[0]
    owner = offset // part_width
    inside = jnp.clip(offset - rep_index * part_width, 0, part_width - tile_width)

    def place(collected, block, source):
        first = source * block_rows
        return lax.dynamic_update_slice_in_dim(collected, block, first, 0)

    empty = jnp.zeros((all_rows, part_width), jnp.float32)

    def advance(shift_count, carry):
        block, collected = carry
        block = shifted(block, "team", 1)
        source = (team_index - shift_count) % team_count
        return (block, place(collected, block, source))

    final = lax.fori_loop(
        1, team_count, advance, (omega_rows, place(empty, omega_rows, team_index))
    )
    collected = final[1]
    partial_value = jnp.dot(
        collected,
        covariance_columns,
        preferred_element_type=jnp.float32,
        precision=lax.Precision.HIGHEST,
    )
    values = lax.dynamic_slice_in_dim(collected, inside, tile_width, 1)
    summed = lax.psum_scatter(partial_value, "rep", scatter_dimension=0, tiled=True)
    everyone = from_root(values, "rep", owner)
    current = lax.dynamic_slice_in_dim(everyone, rep_index * rows_share, rows_share, 0)
    global_rows = rep_index * rows_share + jnp.arange(rows_share, dtype=jnp.int32)
    global_cols = offset + jnp.arange(tile_width, dtype=jnp.int32)
    diagonal = global_rows[:, None] == global_cols[None, :]
    safe = jnp.where(diagonal, current, jnp.float32(1.0))
    gradient = summed - jnp.where(diagonal, 1.0 / safe, jnp.float32(0.0))
    moved = current - step_size * gradient
    shrunk = jnp.sign(moved) * jnp.maximum(jnp.abs(moved) - step_size * penalty, 0.0)
    return jnp.where(diagonal, moved, shrunk)


def solution(mesh):
    in_specs = (P(("groups", "team"), "rep"), P("rep", ("groups", "team")), P(("groups", "team")))
    out_specs = P("rep", ("groups", "team"))
    return jax.shard_map(
        per_device, mesh=mesh, in_specs=in_specs, out_specs=out_specs, check_vma=False
    )
```

profile of v0, /device:TPU:0, one launch (start us, length us, event | category | flops | bytes accessed | tf_op | source)
XLA Modules:
  0.0 114.8 jit_solution(6271310564918737601)
XLA Ops:
  6.5 0.0 all-reduce.2.cloned.1.call-start
  6.5 1.0 copy.18
  8.3 0.1 broadcast_in_dim.13
  8.5 46.3 %while.17 = (s32[]{:T(128)}, f32[16,8192]{1,0:T(8,128)S(1)}, f32[64,8192]{1,0:T(8,128)S(1)}, s32[]{:T(128)}, s32[]{:T(128)}, /*index=5*/s32[]{:T(128)}, s32[]{:T(128)}, s32[]{:T(128)}, s32[]{:T(128)}, s32[]{:T(128)}) while((s32[]{:T(128)}, f32[16,8192]{1,0:T(8,128)S(1)}, f32[64,8192]{1,0:T(8,128)S(1)}, s32[]{:T(128)}, s32[]{:T(128)}, ...), condition=%wide.region_1.2_spmd, body=%wide.region_0.1_spmd.sunk | while | flops 18 | bytes 4194616 | solution.py:45
  8.5 3.1 %collective-permute-start = (f32[16,8192]{1,0:T(8,128)S(1)}, f32[16,8192]{1,0:T(8,128)S(1)}, u32[]{:S(2)}, u32[]{:S(2)}) collective-permute-start(f32[16,8192]{1,0:T(8,128)S(1)} %get-tuple-element.161), channel_id=1, source_target_pairs={{0,4},{4,8},{8,12},{12,0},{1,5},{5,9},{9,13},{13,1},{2,6},{6,10},{... | collective-permute-start | bytes 1572872 | tf_op jit(solution)/shard_map/while/body/eval_jaxpr/ppermute | solution.py:12
  11.5 13.9 %collective-permute-done = f32[16,8192]{1,0:T(8,128)S(1)} collective-permute-done((f32[16,8192]{1,0:T(8,128)S(1)}, f32[16,8192]{1,0:T(8,128)S(1)}, u32[]{:S(2)}, u32[]{:S(2)}) %collective-permute-start) | collective-permute-done | bytes 524320 | tf_op jit(solution)/shard_map/while/body/eval_jaxpr/ppermute | solution.py:12
  25.6 0.1 collective-permute-start
  25.7 14.9 %collective-permute-done = f32[16,8192]{1,0:T(8,128)S(1)} collective-permute-done((f32[16,8192]{1,0:T(8,128)S(1)}, f32[16,8192]{1,0:T(8,128)S(1)}, u32[]{:S(2)}, u32[]{:S(2)}) %collective-permute-start) | collective-permute-done | bytes 524320 | tf_op jit(solution)/shard_map/while/body/eval_jaxpr/ppermute | solution.py:12
  40.7 0.1 collective-permute-start
  40.7 13.9 %collective-permute-done = f32[16,8192]{1,0:T(8,128)S(1)} collective-permute-done((f32[16,8192]{1,0:T(8,128)S(1)}, f32[16,8192]{1,0:T(8,128)S(1)}, u32[]{:S(2)}, u32[]{:S(2)}) %collective-permute-start) | collective-permute-done | bytes 524320 | tf_op jit(solution)/shard_map/while/body/eval_jaxpr/ppermute | solution.py:12
  54.8 0.7 dynamic-slice_select_fusion
  55.5 0.0 all-reduce.2.cloned.1.call-update
  55.5 0.0 reduce-scatter.2.cloned.1.call-start
  55.6 7.3 %fusion.4 = f32[64,256]{1,0:T(8,128)} fusion(f32[64,8192]{1,0:T(8,128)S(1)} %get-tuple-element.116, f32[8192,256]{1,0:T(8,128)} %param.6), kind=kOutput, calls=%fused_computation.12 | convolution fusion | flops 1610612736 | bytes 10551296 | tf_op jit(solution)/shard_map/dot_general | solution.py:49
  62.9 0.0 reduce-scatter.2.cloned.1.call-update
  63.0 21.5 %all-reduce.2.cloned.1.call-done = f32[64,256]{1,0:T(8,128)} async-done(((f32[64,256]{1,0:T(8,128)}), f32[64,256]{1,0:T(8,128)}) %all-reduce.2.cloned.1.call-update) | async-done | bytes 65552 | tf_op jit(solution)/shard_map/psum | solution.py:17
  84.5 22.0 %reduce-scatter.2.cloned.1.call-done = f32[16,256]{1,0:T(8,128)} async-done(((f32[64,256]{1,0:T(8,128)}), f32[16,256]{1,0:T(8,128)}) %reduce-scatter.2.cloned.1.call-update) | async-done | bytes 16400 | tf_op jit(solution)/shard_map/reduce_scatter | solution.py:56
  106.5 1.4 %compare_select_fusion = f32[16,256]{1,0:T(8,128)} fusion(f32[16,256]{1,0:T(8,128)} %reduce-scatter.2.cloned.1.call-done, f32[64,256]{1,0:T(8,128)} %all-reduce.2.cloned.1.call-done, s32[]{:T(128)S(6)} %select_n.64, s32[256]{0:T(256)S(1)} %iota_add_fusion, s32[16]{0:T(128)S(1)} %iota_add_fusion.1), kind=kLoop, calls=%fused_computation.2 | loop fusion | flops 53248 | bytes 50244 | tf_op jit(solution)/shard_map/jit(_where)/select_n | solution.py:66
  (9 shorter events, 0.3 us)
Async XLA Ops:
  6.5 78.0 %all-reduce.2.cloned.1.call-start = ((), (), s32[]{:S(2)}) async-start(), calls=%async_computation.1 | async-start | bytes 131072 | tf_op jit(solution)/shard_map/psum | solution.py:17
  8.5 17.0 %collective-permute-start = (f32[16,8192]{1,0:T(8,128)S(1)}, f32[16,8192]{1,0:T(8,128)S(1)}, u32[]{:S(2)}, u32[]{:S(2)}) collective-permute-start(f32[16,8192]{1,0:T(8,128)S(1)} %get-tuple-element.161), channel_id=1, source_target_pairs={{0,4},{4,8},{8,12},{12,0},{1,5},{5,9},{9,13},{13,1},{2,6},{6,10},{... | collective-permute-start | bytes 1572872 | tf_op jit(solution)/shard_map/while/body/eval_jaxpr/ppermute | solution.py:12
  25.6 15.0 %collective-permute-start = (f32[16,8192]{1,0:T(8,128)S(1)}, f32[16,8192]{1,0:T(8,128)S(1)}, u32[]{:S(2)}, u32[]{:S(2)}) collective-permute-start(f32[16,8192]{1,0:T(8,128)S(1)} %get-tuple-element.161), channel_id=1, source_target_pairs={{0,4},{4,8},{8,12},{12,0},{1,5},{5,9},{9,13},{13,1},{2,6},{6,10},{... | collective-permute-start | bytes 1572872 | tf_op jit(solution)/shard_map/while/body/eval_jaxpr/ppermute | solution.py:12
  40.7 14.0 %collective-permute-start = (f32[16,8192]{1,0:T(8,128)S(1)}, f32[16,8192]{1,0:T(8,128)S(1)}, u32[]{:S(2)}, u32[]{:S(2)}) collective-permute-start(f32[16,8192]{1,0:T(8,128)S(1)} %get-tuple-element.161), channel_id=1, source_target_pairs={{0,4},{4,8},{8,12},{12,0},{1,5},{5,9},{9,13},{13,1},{2,6},{6,10},{... | collective-permute-start | bytes 1572872 | tf_op jit(solution)/shard_map/while/body/eval_jaxpr/ppermute | solution.py:12
  55.5 51.0 %reduce-scatter.2.cloned.1.call-start = ((), (), s32[]{:S(2)}) async-start(), calls=%async_computation.2 | async-start | bytes 81920 | tf_op jit(solution)/shard_map/reduce_scatter | solution.py:56
Sparse Core Ops, SparseCore 0:
  55.7 28.7 all-reduce.1
  87.0 19.4 reduce-scatter.1
where the time goes:
time: 115 us
  waiting for transfers between devices  86.4 us (75%)
  between operations  14.1 us (12%)
  matrix products  7.33 us (6%)
  starting transfers between devices  3.24 us (3%)
  other arithmetic  2.16 us (2%)
  local copies, waits for them, and re-layouts  1.45 us (1%)
    ppermute x3, waiting for transfers between devices, shifted(): lax.ppermute(array, axis, [(i, (i + by) % devices) for i in range(devices)])  42.8 us
    reduce_scatter x1, waiting for transfers between devices, per_device(): lax.psum_scatter(partial_value, 'rep', scatter_dimension=0, tiled=True)  22 us
    psum x1, waiting for transfers between devices, from_root(): return lax.psum(jnp.where(mine, array, jnp.zeros_like(array)), axis)  21.5 us
    dot_general x1, matrix products, per_device(): jnp.dot(collected, covariance_columns, preferred_element_type=jnp.float32...  7.33 us
    ppermute x3, starting transfers between devices, shifted(): lax.ppermute(array, axis, [(i, (i + by) % devices) for i in range(devices)])  3.19 us
  transfers between devices with their start and end apart: 5, of which 5 were waited for; matrix products, arithmetic and copies ran while one was open for 6% of the time, Pallas kernels for 0%

commit v1 on v0

--- a/solution.py
+++ b/solution.py
@@ -14,7 +14,7 @@
 
 def from_root(array, axis, root):
     mine = lax.axis_index(axis) == root
-    return lax.psum(jnp.where(mine, array, jnp.zeros_like(array)), axis)
+    return jnp.sum(lax.all_gather(jnp.where(mine, array, jnp.zeros_like(array)), axis), axis=0)
 
 
 def per_device(omega_rows, covariance_columns, tile_offsets):

time: 115 us -> 87.3 us (0.76)
  waiting for transfers between devices: 86.4 us -> 53.5 us
  blocking collectives: 0 us -> 5.79 us
    psum x1 -> x0, waiting for transfers between devices: 21.5 us -> none  [from_root(): return lax.psum(jnp.where(mine, array, jnp.zeros_like(array)), axis)]
    reduce_scatter x1, waiting for transfers between devices: 22 us -> 10.7 us  [per_device(): lax.psum_scatter(partial_value, 'rep', scatter_dimension=0, tiled=True)]
    all_gather x0 -> x1, blocking collectives: none -> 5.79 us  [from_root(): lax.all_gather(jnp.where(mine, array, jnp.zeros_like(array)), axis)]
  transfers between devices with their start and end apart: 5 -> 4, of which waited for: 5 -> 4; matrix products, arithmetic and copies ran while one was open for 6% -> 0% of each run, Pallas kernels for 0% -> 0%
where the time goes in v1:
time: 87.3 us; the launch traced here: 87 us
  waiting for transfers between devices  53.5 us (61%)
  between operations  14.1 us (16%)
  matrix products  7.32 us (8%)
  blocking collectives  5.79 us (7%)
  starting transfers between devices  3.2 us (4%)
  other arithmetic  1.52 us (2%)
  local copies, waits for them, and re-layouts  1.45 us (2%)
    ppermute x3, waiting for transfers between devices, shifted(): lax.ppermute(array, axis, [(i, (i + by) % devices) for i in range(devices)])  42.8 us
    reduce_scatter x1, waiting for transfers between devices, per_device(): lax.psum_scatter(partial_value, 'rep', scatter_dimension=0, tiled=True)  10.7 us
    dot_general x1, matrix products, per_device(): jnp.dot(collected, covariance_columns, preferred_element_type=jnp.float32...  7.32 us
    all_gather x1, blocking collectives, from_root(): lax.all_gather(jnp.where(mine, array, jnp.zeros_like(array)), axis)  5.79 us
    ppermute x3, starting transfers between devices, shifted(): lax.ppermute(array, axis, [(i, (i + by) % devices) for i in range(devices)])  3.19 us
  transfers between devices with their start and end apart: 4, of which 4 were waited for; matrix products, arithmetic and copies ran while one was open for 0% of the time, Pallas kernels for 0%

profile of v1, /device:TPU:0, one launch (start us, length us, event | category | flops | bytes accessed | tf_op | source)
XLA Modules:
  0.0 87.0 jit_solution(14651481155782846844)
XLA Ops:
  6.5 0.0 reduce-scatter.2.cloned.1.call-start
  6.5 1.0 %copy.17 = f32[16,8192]{1,0:T(8,128)S(1)} copy(f32[16,8192]{1,0:T(8,128)} %param.5) | data formatting | bytes 1048576
  7.6 0.1 broadcast_in_dim.13
  7.8 46.3 %while.17 = (s32[]{:T(128)}, f32[16,8192]{1,0:T(8,128)S(1)}, f32[64,8192]{1,0:T(8,128)S(1)}, s32[]{:T(128)}, s32[]{:T(128)}, /*index=5*/s32[]{:T(128)}, s32[]{:T(128)}, s32[]{:T(128)}, s32[]{:T(128)}, s32[]{:T(128)}) while((s32[]{:T(128)}, f32[16,8192]{1,0:T(8,128)S(1)}, f32[64,8192]{1,0:T(8,128)S(1)}, s32[]{:T(128)}, s32[]{:T(128)}, ...), condition=%wide.region_1.2_spmd, body=%wide.region_0.1_spmd.sunk | while | flops 18 | bytes 4194616 | solution.py:45
  7.8 3.1 %collective-permute-start = (f32[16,8192]{1,0:T(8,128)S(1)}, f32[16,8192]{1,0:T(8,128)S(1)}, u32[]{:S(2)}, u32[]{:S(2)}) collective-permute-start(f32[16,8192]{1,0:T(8,128)S(1)} %get-tuple-element.161), channel_id=1, source_target_pairs={{0,4},{4,8},{8,12},{12,0},{1,5},{5,9},{9,13},{13,1},{2,6},{6,10},{... | collective-permute-start | bytes 1572872 | tf_op jit(solution)/shard_map/while/body/eval_jaxpr/ppermute | solution.py:12
  10.9 13.9 %collective-permute-done = f32[16,8192]{1,0:T(8,128)S(1)} collective-permute-done((f32[16,8192]{1,0:T(8,128)S(1)}, f32[16,8192]{1,0:T(8,128)S(1)}, u32[]{:S(2)}, u32[]{:S(2)}) %collective-permute-start) | collective-permute-done | bytes 524320 | tf_op jit(solution)/shard_map/while/body/eval_jaxpr/ppermute | solution.py:12
  24.9 0.1 collective-permute-start
  25.0 14.9 %collective-permute-done = f32[16,8192]{1,0:T(8,128)S(1)} collective-permute-done((f32[16,8192]{1,0:T(8,128)S(1)}, f32[16,8192]{1,0:T(8,128)S(1)}, u32[]{:S(2)}, u32[]{:S(2)}) %collective-permute-start) | collective-permute-done | bytes 524320 | tf_op jit(solution)/shard_map/while/body/eval_jaxpr/ppermute | solution.py:12
  40.0 0.1 collective-permute-start
  40.1 13.9 %collective-permute-done = f32[16,8192]{1,0:T(8,128)S(1)} collective-permute-done((f32[16,8192]{1,0:T(8,128)S(1)}, f32[16,8192]{1,0:T(8,128)S(1)}, u32[]{:S(2)}, u32[]{:S(2)}) %collective-permute-start) | collective-permute-done | bytes 524320 | tf_op jit(solution)/shard_map/while/body/eval_jaxpr/ppermute | solution.py:12
  54.1 7.3 %fusion.4 = f32[64,256]{1,0:T(8,128)} fusion(f32[64,8192]{1,0:T(8,128)S(1)} %get-tuple-element.116, f32[8192,256]{1,0:T(8,128)} %param.6), kind=kOutput, calls=%fused_computation.12 | convolution fusion | flops 1610612736 | bytes 10551296 | tf_op jit(solution)/shard_map/dot_general | solution.py:49
  61.4 0.0 reduce-scatter.2.cloned.1.call-update
  62.1 0.1 dynamic-slice_select_fusion
  62.2 5.8 %all-gather = f32[256,256]{1,0:T(8,128)S(1)} all-gather(f32[64,256]{1,0:T(8,128)S(1)} %dynamic-slice_select_fusion), channel_id=2, replica_groups=mesh['groups'=2,'team'=4,'rep'=4] {'rep'}, dimensions={0}, use_global_device_ids=true | all-gather | bytes 327680 | tf_op jit(solution)/shard_map/all_gather | solution.py:17
  68.1 10.7 %reduce-scatter.2.cloned.1.call-done = f32[16,256]{1,0:T(8,128)} async-done(((f32[64,256]{1,0:T(8,128)}), f32[16,256]{1,0:T(8,128)}) %reduce-scatter.2.cloned.1.call-update) | async-done | bytes 16400 | tf_op jit(solution)/shard_map/reduce_scatter | solution.py:56
  78.7 1.4 %compare_select_fusion = f32[16,256]{1,0:T(8,128)} fusion(f32[16,256]{1,0:T(8,128)} %reduce-scatter.2.cloned.1.call-done, f32[64,256]{1,0:T(8,128)S(1)} %reduce_sum.9, s32[]{:T(128)S(6)} %select_n.64, s32[256]{0:T(256)S(1)} %iota_add_fusion, s32[16]{0:T(128)S(1)} %iota_add_fusion.1), kind=kLoop, calls=%fused_computation.2 | loop fusion | flops 53248 | bytes 50244 | tf_op jit(solution)/shard_map/jit(_where)/select_n | solution.py:66
  (10 shorter events, 0.3 us)
Async XLA Ops:
  6.5 72.2 %reduce-scatter.2.cloned.1.call-start = ((), (), s32[]{:S(2)}) async-start(), calls=%async_computation.1 | async-start | bytes 81920 | tf_op jit(solution)/shard_map/reduce_scatter | solution.py:56
  7.8 17.0 %collective-permute-start = (f32[16,8192]{1,0:T(8,128)S(1)}, f32[16,8192]{1,0:T(8,128)S(1)}, u32[]{:S(2)}, u32[]{:S(2)}) collective-permute-start(f32[16,8192]{1,0:T(8,128)S(1)} %get-tuple-element.161), channel_id=1, source_target_pairs={{0,4},{4,8},{8,12},{12,0},{1,5},{5,9},{9,13},{13,1},{2,6},{6,10},{... | collective-permute-start | bytes 1572872 | tf_op jit(solution)/shard_map/while/body/eval_jaxpr/ppermute | solution.py:12
  24.9 15.0 %collective-permute-start = (f32[16,8192]{1,0:T(8,128)S(1)}, f32[16,8192]{1,0:T(8,128)S(1)}, u32[]{:S(2)}, u32[]{:S(2)}) collective-permute-start(f32[16,8192]{1,0:T(8,128)S(1)} %get-tuple-element.161), channel_id=1, source_target_pairs={{0,4},{4,8},{8,12},{12,0},{1,5},{5,9},{9,13},{13,1},{2,6},{6,10},{... | collective-permute-start | bytes 1572872 | tf_op jit(solution)/shard_map/while/body/eval_jaxpr/ppermute | solution.py:12
  40.0 14.0 %collective-permute-start = (f32[16,8192]{1,0:T(8,128)S(1)}, f32[16,8192]{1,0:T(8,128)S(1)}, u32[]{:S(2)}, u32[]{:S(2)}) collective-permute-start(f32[16,8192]{1,0:T(8,128)S(1)} %get-tuple-element.161), channel_id=1, source_target_pairs={{0,4},{4,8},{8,12},{12,0},{1,5},{5,9},{9,13},{13,1},{2,6},{6,10},{... | collective-permute-start | bytes 1572872 | tf_op jit(solution)/shard_map/while/body/eval_jaxpr/ppermute | solution.py:12
Sparse Core Ops, SparseCore 0:
  61.6 17.1 reduce-scatter.1
